TPU v7x, 128 devices: a whole 4x4x4 slice. The times are simulated.
128 devices in a mesh: gx: 16 (over y, x), gy: 8 (over z, core).
Axes of the slice: x: 4, y: 4, z: 4, core: 2. Of those that a mesh axis runs over, the one named last changes fastest.
Arguments:
- volume: bfloat16 [96, 64, 128, 128], P('gx', None, 'gy'), may hold values from -6 to 6
- weight3: bfloat16 [128, 27, 64], replicated, may hold values from -0.15625 to 0.15625
- bias3: bfloat16 [128], replicated, may hold values from -4 to 4
- weight4: bfloat16 [256, 27, 128], P('gy', None, 'gx'), may hold values from -0.109375 to 0.109375
- bias4: bfloat16 [256], P('gy'), may hold values from -3 to 3
Outputs:
- encoded: bfloat16 [48, 256, 4096], P('gx', 'gy')
All inputs are finite; a program needn't handle non-finite values.
Results may differ from a plain program's by a relative error of at most 0.015.
Values may be sent and summed in bfloat16 or wider, within the bound.
A program may use at most 384 MiB of HBM per device.

v0:
```python
import jax
import jax.numpy as jnp
from jax import lax
from jax.sharding import PartitionSpec as P


def with_halo(block, sides, width):
    for axis, dim in sides:
        count = lax.axis_size(axis)
        forward = [(i, i + 1) for i in range(count - 1)]
        backward = [(target, source) for source, target in forward]
        low = lax.ppermute(
            lax.slice_in_dim(block, block.shape[dim] - width, None, axis=dim), axis, forward
        )
        high = lax.ppermute(lax.slice_in_dim(block, 0, width, axis=dim), axis, backward)
        block = jnp.concatenate([low, block, high], axis=dim)
    return block


def block_conv(padded, weight):
    outs = weight.shape[0]
    ins = weight.shape[2]
    kernel = weight.reshape(outs, 3, 3, 3, ins)
    result = lax.conv_general_dilated(
        padded[None],
        kernel,
        (1, 1, 1),
        "VALID",
        dimension_numbers=("NDCHW", "ODHWI", "NDCHW"),
        preferred_element_type=jnp.float32,
    )
    return result[0]


def leaky_round(values):
    return jnp.where(values > 0, values, 0.3 * values).astype(jnp.bfloat16)


def on_device(volume, weight3, bias3, weight4, bias4):
    planes, in_chans, rows, side = volume.shape
    out_chans = weight3.shape[0]
    extended = with_halo(volume, (("gx", 0), ("gy", 2)), 1)
    padded3 = jnp.pad(extended, ((0, 0), (0, 0), (0, 0), (1, 1)))
    half_rows = rows // 2
    half_side = side // 2
    slab = planes // 2
    result3 = block_conv(padded3, weight3) + bias3.astype(jnp.float32)[None, :, None, None]
    active = jnp.maximum(result3, 0.0).reshape(slab, 2, out_chans, half_rows, 2, half_side, 2)
    pooled = jnp.max(active, axis=(1, 4, 6)).astype(jnp.bfloat16)
    kernel_in = lax.all_gather(weight4, "gx", axis=2, tiled=True)
    kernel_all, bias_all = (
        lax.all_gather(kernel_in, "gy", axis=0, tiled=True),
        lax.all_gather(bias4, "gy", axis=0, tiled=True),
    )
    all_outs = kernel_all.shape[0]
    rimmed = with_halo(pooled, (("gx", 0), ("gy", 2)), 1)
    padded4 = jnp.pad(rimmed, ((0, 0), (0, 0), (0, 0), (1, 1)))
    result = block_conv(padded4, kernel_all).reshape(slab, all_outs, half_rows * half_side)
    local = leaky_round(result + bias_all.astype(jnp.float32)[None, :, None])
    encoded = lax.all_to_all(local, "gy", split_axis=1, concat_axis=2, tiled=True)
    return encoded


def solution(mesh):
    return jax.shard_map(
        on_device,
        mesh=mesh,
        in_specs=(P("gx", None, "gy", None), P(), P(), P("gy", None, "gx"), P("gy")),
        out_specs=P("gx", "gy", None),
        check_vma=False,
    )
```

profile of v0, /device:TPU:1, one launch (start us, length us, event | category | flops | bytes accessed | tf_op | source)
XLA Modules:
  0.0 155.4 jit_solution(9364337676811580483)
XLA Ops:
  6.5 1.1 fusion.40
  7.7 4.0 %collective-permute-start = (bf16[1,64,16,128]{3,2,1,0:T(8,128)(2,1)S(1)}, bf16[1,64,16,128]{3,2,1,0:T(8,128)(2,1)S(1)}, u32[]{:S(2)}, u32[]{:S(2)}) collective-permute-start(bf16[1,64,16,128]{3,2,1,0:T(8,128)(2,1)S(1)} %get-tuple-element.7), channel_id=1, source_target_pairs={{0,8},{8,16},{16,24},{24,32},{32,40},{40,48},{48,56},{56,64},{64,7... | collective-permute-start | bytes 786440 | tf_op jit(solution)/shard_map/ppermute | solution.py:12
  11.6 1.3 collective-permute-start.1
  12.9 5.2 %copy.46 = bf16[6,64,16,128]{1,0,3,2:T(8,128)(2,1)} copy(bf16[6,64,16,128]{3,2,1,0:T(8,128)(2,1)} %param.5) | data formatting | bytes 3145728 | tf_op args[0]
  18.1 0.6 copy.45
  18.8 1.6 %collective-permute-done.1 = bf16[1,64,16,128]{3,2,1,0:T(8,128)(2,1)S(1)} collective-permute-done((bf16[1,64,16,128]{3,2,1,0:T(8,128)(2,1)S(1)}, bf16[1,64,16,128]{3,2,1,0:T(8,128)(2,1)S(1)}, u32[]{:S(2)}, u32[]{:S(2)}) %collective-permute-start.1) | collective-permute-done | bytes 262176 | tf_op jit(solution)/shard_map/ppermute | solution.py:15
  20.4 0.6 copy.47
  21.1 2.4 %pad_maximum_fusion.2 = (bf16[8,64,1,128]{1,0,3,2:T(8,128)(2,1)}, bf16[8,64,1,128]{1,0,3,2:T(8,128)(2,1)}) fusion(bf16[1,64,16,128]{1,0,3,2:T(2,128)(2,1)S(1)} %copy.47, bf16[6,64,16,128]{1,0,3,2:T(8,128)(2,1)} %copy.46, bf16[1,64,16,128]{1,0,3,2:T(2,128)(2,1)S(1)} %copy.45), kind=kLoop, calls=%fused_computation.47 | loop fusion | flops 786432 | bytes 2359296 | tf_op jit(solution)/shard_map/slice | solution.py:13
  23.4 5.3 %collective-permute-start.2 = (bf16[8,64,1,128]{1,0,3,2:T(8,128)(2,1)}, bf16[8,64,1,128]{1,0,3,2:T(8,128)(2,1)}, u32[]{:S(2)}, u32[]{:S(2)}) collective-permute-start(bf16[8,64,1,128]{1,0,3,2:T(8,128)(2,1)} %get-tuple-element.5), channel_id=1, source_target_pairs={{0,1},{1,2},{2,3},{3,4},{4,5},{5,6},{6,7},{8,9},{9,10},{10,11},{11... | collective-permute-start | bytes 393224 | tf_op jit(solution)/shard_map/ppermute | solution.py:12
  28.7 1.9 %collective-permute-start.3 = (bf16[8,64,1,128]{1,0,3,2:T(8,128)(2,1)}, bf16[8,64,1,128]{1,0,3,2:T(8,128)(2,1)}, u32[]{:S(2)}, u32[]{:S(2)}) collective-permute-start(bf16[8,64,1,128]{1,0,3,2:T(8,128)(2,1)} %get-tuple-element.6), channel_id=1, source_target_pairs={{1,0},{2,1},{3,2},{4,3},{5,4},{6,5},{7,6},{9,8},{10,9},{11,10},{12... | collective-permute-start | bytes 393224 | tf_op jit(solution)/shard_map/ppermute | solution.py:15
  30.7 22.8 %all_gather.9 = bf16[32,27,128]{0,2,1:T(8,128)(2,1)S(1)} all-gather(bf16[32,27,8]{0,2,1:T(8,128)(2,1)S(1)} %copy-done.1), channel_id=1, replica_groups=mesh['gx'=16,'gy'=8] {'gx'}, dimensions={2}, use_global_device_ids=true | all-gather | bytes 235008 | tf_op jit(solution)/shard_map/all_gather | solution.py:50
  53.5 1.0 copy.54
  54.5 0.0 all-gather.2.cloned.1.call-update
  54.5 7.9 %fusion.9 = bf16[8,64,18,1,130]{1,0,4,2,3:T(8,128)(2,1)S(1)} fusion(bf16[8,64,1,128]{1,0,3,2:T(8,128)(2,1)} %collective-permute-done.3, bf16[8,64,1,128]{1,0,3,2:T(8,128)(2,1)} %collective-permute-done.2, bf16[1,64,16,128]{1,0,3,2:T(2,128)(2,1)S(1)} %copy.47, bf16[6,64,16,128]{1,0,3,2:T(8,128)(2,1)} %copy.46, bf16[1,64,16,128]{1,0,3,2:T(2,128)(2,1)S(1)} %copy.45), kind=kLoop, calls=%fused_computation.13 | loop fusion | flops 21565440 | bytes 4755456 | tf_op jit(solution)/shard_map/broadcast_in_dim | solution.py:25
  62.5 1.3 pad.10
  63.8 0.0 copy-start.5
  63.8 0.6 copy.49
  64.5 0.2 slice.36
  64.7 12.9 %broadcast_select_fusion = f32[6,16,8,17,128]{4,2,3,1,0:T(8,128)S(1)} fusion(pred[8,17]{0,1:T(8,128)(4,1)S(1)} %copy-done.5, bf16[128,3,3,3,64]{0,4,3,2,1:T(8,128)(2,1)S(1)} %bitcast.32, bf16[8,64,18,1,7,2]{1,4,5,2,0,3:T(8,128)(2,1)S(1)} %slice.36, bf16[8,64,18,1,8,17]{1,4,5,2,0,3:T(8,128)(2,1)S(1)} %copy.49), kind=kOutput, calls=%fused_computation.23 | convolution fusion | flops 5785632768 | bytes 9891976 | tf_op jit(solution)/shard_map/conv_general_dilated | solution.py:24
  77.6 1.1 copy.50
  78.7 0.4 slice.37
  79.2 0.0 copy-start.4
  79.2 5.5 %maximum_reduce_fusion = bf16[3,128,8,64]{1,2,3,0:T(8,128)(2,1)S(1)} fusion(f32[3,2,128,8,2,64,2]{2,4,3,6,5,1,0:T(2,128)S(1)} %bitcast.34, f32[128]{0:T(128)S(1)} %convert_element_type.16), kind=kLoop, calls=%fused_computation.5 | loop fusion | flops 4521984 | bytes 6685184 | tf_op jit(solution)/shard_map/reduce_max | solution.py:49
  84.7 1.8 %collective-permute-start.4 = (bf16[1,128,8,64]{1,2,3,0:T(8,128)(2,1)S(1)}, bf16[1,128,8,64]{1,2,3,0:T(8,128)(2,1)S(1)}, u32[]{:S(2)}, u32[]{:S(2)}) collective-permute-start(bf16[1,128,8,64]{1,2,3,0:T(8,128)(2,1)S(1)} %get-tuple-element.11), channel_id=1, source_target_pairs={{0,8},{8,16},{16,24},{24,32},{32,40},{40,48},{48,56},{56,64},{64,7... | collective-permute-start | bytes 393224 | tf_op jit(solution)/shard_map/ppermute | solution.py:12
  86.5 1.3 collective-permute-start.5
  87.8 0.6 collective-permute-done.4
  88.4 3.8 %collective-permute-done.5 = bf16[1,128,8,64]{1,2,3,0:T(8,128)(2,1)S(1)} collective-permute-done((bf16[1,128,8,64]{1,2,3,0:T(8,128)(2,1)S(1)}, bf16[1,128,8,64]{1,2,3,0:T(8,128)(2,1)S(1)}, u32[]{:S(2)}, u32[]{:S(2)}) %collective-permute-start.5) | collective-permute-done | bytes 131104 | tf_op jit(solution)/shard_map/ppermute | solution.py:15
  92.2 0.2 pad_maximum_fusion.5
  92.4 10.7 %collective-permute-start.6 = (bf16[5,128,1,64]{1,2,3,0:T(2,128)(2,1)S(1)}, bf16[5,128,1,64]{1,2,3,0:T(2,128)(2,1)S(1)}, u32[]{:S(2)}, u32[]{:S(2)}) collective-permute-start(bf16[5,128,1,64]{1,2,3,0:T(2,128)(2,1)S(1)} %get-tuple-element.9), channel_id=1, source_target_pairs={{0,1},{1,2},{2,3},{3,4},{4,5},{5,6},{6,7},{8,9},{9,10},{10,11},{11... | collective-permute-start | bytes 245768 | tf_op jit(solution)/shard_map/ppermute | solution.py:12
  103.1 1.9 %collective-permute-start.7 = (bf16[5,128,1,64]{1,2,3,0:T(2,128)(2,1)S(1)}, bf16[5,128,1,64]{1,2,3,0:T(2,128)(2,1)S(1)}, u32[]{:S(2)}, u32[]{:S(2)}) collective-permute-start(bf16[5,128,1,64]{1,2,3,0:T(2,128)(2,1)S(1)} %get-tuple-element.10), channel_id=1, source_target_pairs={{1,0},{2,1},{3,2},{4,3},{5,4},{6,5},{7,6},{9,8},{10,9},{11,10},{12... | collective-permute-start | bytes 245768 | tf_op jit(solution)/shard_map/ppermute | solution.py:15
  105.0 0.6 dynamic-slice
  106.3 0.2 dynamic-update-slice
  106.5 12.5 %all-reduce.2 = bf16[256]{0:T(256)(128)(2,1)S(1)} all-reduce(bf16[256]{0:T(256)(128)(2,1)S(1)} %dynamic-update-slice), channel_id=1, replica_groups=mesh['gx'=16,'gy'=8] {'gy'}, use_global_device_ids=true, to_apply=%add.2 | all-reduce | flops 256 | bytes 1024
  119.1 0.8 fusion.21
  119.9 0.3 pad.12
  120.2 0.2 copy.53
  120.4 0.1 slice.40
  120.5 0.0 all-gather.2.cloned.1.call-done
  120.5 0.1 copy-done.6
  120.6 5.0 %convolution_select_fusion = f32[3,8,8,9,256]{4,2,3,1,0:T(8,128)S(1)} fusion(bf16[256,3,3,3,128]{4,0,3,2,1:T(8,128)(2,1)} %bitcast.40, bf16[5,128,10,1,7,2]{1,4,5,2,0,3:T(8,128)(2,1)S(1)} %slice.40, bf16[5,128,10,1,8,9]{1,4,5,2,0,3:T(8,128)(2,1)S(1)} %copy.53, pred[8,9]{0,1:T(8,128)(4,1)S(1)} %copy-done.6), kind=kOutput, calls=%fused_computation.30 | convolution fusion | flops 3061469184 | bytes 4639816 | tf_op jit(solution)/shard_map/conv_general_dilated | solution.py:24
  125.6 0.6 copy.55
  126.2 0.1 slice_bitcast_fusion
  126.3 0.5 copy.56
  126.9 0.2 fusion.20
  127.1 1.0 copy.57
  128.1 19.3 %all_to_all.18 = bf16[3,256,512]{2,0,1:T(4,128)(2,1)S(1)} all-to-all(bf16[3,256,512]{2,0,1:T(4,128)(2,1)S(1)} %copy.57), channel_id=1, replica_groups=mesh['gx'=16,'gy'=8] {'gy'}, dimensions={1} | all-to-all | bytes 1572864 | tf_op jit(solution)/shard_map/all_to_all | solution.py:60
  147.4 0.2 copy.58
  147.6 1.0 copy.62
  (21 shorter events, 0.1 us)
Async XLA Ops:
  6.5 58.1 %copy-start = (bf16[128,27,64]{0,2,1:T(8,128)(2,1)S(1)}, bf16[128,27,64]{0,2,1:T(8,128)(2,1)}, u32[]{:S(2)}) copy-start(bf16[128,27,64]{0,2,1:T(8,128)(2,1)} %param.6) | copy-start | bytes 1327108
  6.5 114.0 %all-gather.2.cloned.1.call-start = ((), (), s32[]{:S(2)}) async-start(), calls=%async_computation.1 | async-start | bytes 1990656 | tf_op jit(solution)/shard_map/all_gather | solution.py:52
  7.7 10.5 %collective-permute-start = (bf16[1,64,16,128]{3,2,1,0:T(8,128)(2,1)S(1)}, bf16[1,64,16,128]{3,2,1,0:T(8,128)(2,1)S(1)}, u32[]{:S(2)}, u32[]{:S(2)}) collective-permute-start(bf16[1,64,16,128]{3,2,1,0:T(8,128)(2,1)S(1)} %get-tuple-element.7), channel_id=1, source_target_pairs={{0,8},{8,16},{16,24},{24,32},{32,40},{40,48},{48,56},{56,64},{64,7... | collective-permute-start | bytes 786440 | tf_op jit(solution)/shard_map/ppermute | solution.py:12
  11.6 8.8 %collective-permute-start.1 = (bf16[1,64,16,128]{3,2,1,0:T(8,128)(2,1)S(1)}, bf16[1,64,16,128]{3,2,1,0:T(8,128)(2,1)S(1)}, u32[]{:S(2)}, u32[]{:S(2)}) collective-permute-start(bf16[1,64,16,128]{3,2,1,0:T(8,128)(2,1)S(1)} %get-tuple-element.8), channel_id=1, source_target_pairs={{8,0},{16,8},{24,16},{32,24},{40,32},{48,40},{56,48},{64,56},{72,6... | collective-permute-start | bytes 786440 | tf_op jit(solution)/shard_map/ppermute | solution.py:15
  21.0 9.6 %copy-start.1 = (bf16[32,27,8]{0,2,1:T(8,128)(2,1)S(1)}, bf16[32,27,8]{0,2,1:T(8,128)(2,1)}, u32[]{:S(2)}) copy-start(bf16[32,27,8]{0,2,1:T(8,128)(2,1)} %param.8) | copy-start | bytes 41476
  21.0 33.5 %copy-start.2 = (bf16[128]{0:T(256)(128)(2,1)S(1)}, bf16[128]{0:T(256)(128)(2,1)}, u32[]{:S(2)}) copy-start(bf16[128]{0:T(256)(128)(2,1)} %param.7) | copy-start | bytes 772
  23.4 31.1 %collective-permute-start.2 = (bf16[8,64,1,128]{1,0,3,2:T(8,128)(2,1)}, bf16[8,64,1,128]{1,0,3,2:T(8,128)(2,1)}, u32[]{:S(2)}, u32[]{:S(2)}) collective-permute-start(bf16[8,64,1,128]{1,0,3,2:T(8,128)(2,1)} %get-tuple-element.5), channel_id=1, source_target_pairs={{0,1},{1,2},{2,3},{3,4},{4,5},{5,6},{6,7},{8,9},{9,10},{10,11},{11... | collective-permute-start | bytes 393224 | tf_op jit(solution)/shard_map/ppermute | solution.py:12
  28.7 25.8 %collective-permute-start.3 = (bf16[8,64,1,128]{1,0,3,2:T(8,128)(2,1)}, bf16[8,64,1,128]{1,0,3,2:T(8,128)(2,1)}, u32[]{:S(2)}, u32[]{:S(2)}) collective-permute-start(bf16[8,64,1,128]{1,0,3,2:T(8,128)(2,1)} %get-tuple-element.6), channel_id=1, source_target_pairs={{1,0},{2,1},{3,2},{4,3},{5,4},{6,5},{7,6},{9,8},{10,9},{11,10},{12... | collective-permute-start | bytes 393224 | tf_op jit(solution)/shard_map/ppermute | solution.py:15
  63.8 0.8 copy-start.5
  79.2 25.9 %copy-start.4 = (u32[128]{0:T(128)S(1)}, u32[128]{0:T(128)}, u32[]{:S(2)}) copy-start(u32[128]{0:T(128)} %constant.28) | copy-start | bytes 1540
  79.2 27.1 %copy-start.3 = (bf16[32]{0:T(256)(128)(2,1)S(1)}, bf16[32]{0:T(256)(128)(2,1)}, u32[]{:S(2)}) copy-start(bf16[32]{0:T(256)(128)(2,1)} %param.9) | copy-start | bytes 196
  84.7 3.7 %collective-permute-start.4 = (bf16[1,128,8,64]{1,2,3,0:T(8,128)(2,1)S(1)}, bf16[1,128,8,64]{1,2,3,0:T(8,128)(2,1)S(1)}, u32[]{:S(2)}, u32[]{:S(2)}) collective-permute-start(bf16[1,128,8,64]{1,2,3,0:T(8,128)(2,1)S(1)} %get-tuple-element.11), channel_id=1, source_target_pairs={{0,8},{8,16},{16,24},{24,32},{32,40},{40,48},{48,56},{56,64},{64,7... | collective-permute-start | bytes 393224 | tf_op jit(solution)/shard_map/ppermute | solution.py:12
  86.5 5.7 %collective-permute-start.5 = (bf16[1,128,8,64]{1,2,3,0:T(8,128)(2,1)S(1)}, bf16[1,128,8,64]{1,2,3,0:T(8,128)(2,1)S(1)}, u32[]{:S(2)}, u32[]{:S(2)}) collective-permute-start(bf16[1,128,8,64]{1,2,3,0:T(8,128)(2,1)S(1)} %get-tuple-element.12), channel_id=1, source_target_pairs={{8,0},{16,8},{24,16},{32,24},{40,32},{48,40},{56,48},{64,56},{72,6... | collective-permute-start | bytes 393224 | tf_op jit(solution)/shard_map/ppermute | solution.py:15
  92.4 26.7 %collective-permute-start.6 = (bf16[5,128,1,64]{1,2,3,0:T(2,128)(2,1)S(1)}, bf16[5,128,1,64]{1,2,3,0:T(2,128)(2,1)S(1)}, u32[]{:S(2)}, u32[]{:S(2)}) collective-permute-start(bf16[5,128,1,64]{1,2,3,0:T(2,128)(2,1)S(1)} %get-tuple-element.9), channel_id=1, source_target_pairs={{0,1},{1,2},{2,3},{3,4},{4,5},{5,6},{6,7},{8,9},{9,10},{10,11},{11... | collective-permute-start | bytes 245768 | tf_op jit(solution)/shard_map/ppermute | solution.py:12
  103.1 16.0 %collective-permute-start.7 = (bf16[5,128,1,64]{1,2,3,0:T(2,128)(2,1)S(1)}, bf16[5,128,1,64]{1,2,3,0:T(2,128)(2,1)S(1)}, u32[]{:S(2)}, u32[]{:S(2)}) collective-permute-start(bf16[5,128,1,64]{1,2,3,0:T(2,128)(2,1)S(1)} %get-tuple-element.10), channel_id=1, source_target_pairs={{1,0},{2,1},{3,2},{4,3},{5,4},{6,5},{7,6},{9,8},{10,9},{11,10},{12... | collective-permute-start | bytes 245768 | tf_op jit(solution)/shard_map/ppermute | solution.py:15
  119.9 0.7 copy-start.6
Sparse Core Ops, SparseCore 0:
  54.6 30.0 all-gather.1
where the time goes:
time: 159 us; the launch traced here: 155 us
  blocking collectives  54.7 us (34%)
  starting transfers between devices  28.1 us (18%)
  matrix products  17.9 us (11%)
  local copies, waits for them, and re-layouts  17.1 us (11%)
  other arithmetic  17.1 us (11%)
  between operations  14.4 us (9%)
  waiting for transfers between devices  6.06 us (4%)
    all_gather x1, blocking collectives, on_device(): kernel_in = lax.all_gather(weight4, 'gx', axis=2, tiled=True)  22.8 us
    ppermute x4, starting transfers between devices, with_halo(): lax.ppermute(lax.slice_in_dim(block, block.shape[dim] - width, None, axis...  21.7 us
    all_to_all x1, blocking collectives, on_device(): lax.all_to_all(local, 'gy', split_axis=1, concat_axis=2, tiled=True)  19.3 us
    conv_general_dilated x2, matrix products, block_conv(): lax.conv_general_dilated(padded[None], kernel, (1, 1, 1), 'VALID', dimens...  17.9 us
    unnamed x1, blocking collectives  12.5 us
    broadcast_in_dim x2, other arithmetic, block_conv(): padded[None]  8.73 us
    ppermute x4, starting transfers between devices, with_halo(): lax.ppermute(lax.slice_in_dim(block, 0, width, axis=dim), axis, backward)  6.43 us
    unnamed x18, local copies, waits for them, and re-layouts  6.14 us
  transfers between devices with their start and end apart: 9, of which 3 were waited for; matrix products, arithmetic and copies ran while one was open for 25% of the time, Pallas kernels for 0%

commit v1 on v0

v1 whole, which is shorter than its diff:
```python
import jax
import jax.numpy as jnp
from jax import lax
from jax.experimental import pallas as pl
from jax.experimental.pallas import tpu as pltpu
from jax.sharding import PartitionSpec as P

MESH = pl.DeviceIdType.MESH
F32 = jnp.float32
BF16 = jnp.bfloat16
NT = (((1,), (1,)), ((), ()))
NX = 16
NY = 8


def remote(src, dst, send, recv, gx, gy):
    return pltpu.make_async_remote_copy(
        src_ref=src, dst_ref=dst, send_sem=send, recv_sem=recv, device_id=(gx, gy), device_id_type=MESH
    )


def loop(count, step):
    lax.fori_loop(0, count, lambda i, c: (step(i), c)[1], 0)


def kernel(
    vol, w3, b3, w4, b4, out,
    v, rh, vs, tt, xt, rr, w3f, w3n, x4, ph, pr, pt, ws, ga, ff, wk, ob,
    lsem, hs, hr, rs, rrs, as_, ar, bs, br, fs, fr, phs, phr, prs, prr, os_, or_, ol,
):
    gx = lax.axis_index("gx")
    gy = lax.axis_index("gy")
    xup, xdn = lax.rem(gx + 1, NX), lax.rem(gx + NX - 1, NX)
    yup, ydn = lax.rem(gy + 1, NY), lax.rem(gy + NY - 1, NY)
    sib = gy + 1 - 2 * lax.rem(gy, 2)
    has_xdn = (gx > 0).astype(F32)
    has_xup = (gx < NX - 1).astype(F32)
    has_ydn = (gy > 0).astype(F32)
    has_yup = (gy < NY - 1).astype(F32)

    barrier = pltpu.get_barrier_semaphore()

    def greet_x(k):
        pl.semaphore_signal(barrier, inc=1, device_id=(lax.rem(gx + k + 1, NX), gy), device_id_type=MESH)

    def greet_y(k):
        pl.semaphore_signal(barrier, inc=1, device_id=(gx, lax.rem(gy + k + 1, NY)), device_id_type=MESH)

    loop(NX - 1, greet_x)
    loop(NY - 1, greet_y)
    local_vol = pltpu.make_async_copy(vol, v, lsem)
    local_vol.start()

    ws[...] = jnp.zeros_like(ws)
    for o in range(32):
        ws[o * 32 : o * 32 + 27, 0:8] = w4[o].astype(F32)
    eye = lax.broadcasted_iota(jnp.int32, (32, 32), 0) == lax.broadcasted_iota(jnp.int32, (32, 32), 1)
    bcol = jnp.sum(jnp.where(eye, b4[...].astype(F32), 0.0), axis=1, keepdims=True)
    lane0 = lax.broadcasted_iota(jnp.int32, (32, 128), 1) == 0
    ws[pl.ds(27, 32, 32), :] = jnp.where(lane0, bcol, 0.0)
    row = lax.broadcasted_iota(jnp.int32, (128, 128), 0)
    col = lax.broadcasted_iota(jnp.int32, (128, 128), 1)
    spread = jnp.where((col % 8 == row), 1.0, 0.0).astype(BF16)
    rep = lax.dot_general(ws[...].astype(BF16), spread, (((1,), (0,)), ((), ())), preferred_element_type=F32)
    rep = rep.reshape(2, 16, 32, 128)
    group = lax.broadcasted_iota(jnp.int32, (2, 32, 128), 2) // 8
    packed = jnp.zeros((2, 32, 128), F32)
    for b in range(16):
        packed = packed + jnp.where(group == b, rep[:, b], 0.0)
    ga[gx] = packed.reshape(64, 128).astype(BF16)

    pl.semaphore_wait(barrier, NX - 1 + NY - 1)

    plane_up = remote(vol.at[5], rh.at[0], hs.at[0], hr.at[0], xup, gy)
    plane_dn = remote(vol.at[0], rh.at[1], hs.at[1], hr.at[1], xdn, gy)
    plane_up.start()
    plane_dn.start()

    def gather_x(k):
        return remote(ga.at[gx], ga.at[gx], as_.at[k], ar.at[k], lax.rem(gx + k + 1, NX), gy)

    def gather_x_in(k):
        src = lax.rem(gx + NX - k - 1, NX)
        return remote(ga.at[src], ga.at[src], as_.at[k], ar.at[k], gx, gy)

    loop(NX - 1, lambda k: gather_x(k).start())

    w3f[...] = jnp.zeros_like(w3f)

    def widen(o):
        w3f[pl.ds(o * 32, 27), 0:64] = w3[o].astype(F32)

    loop(128, widen)
    for n in range(9):
        k0, k1, k2 = (w3f[pl.ds(9 * kd + n, 128, 32), :][:, 0:64] for kd in range(3))
        z = jnp.zeros((128, 64), F32)
        w3n[0:128, n * 256 : n * 256 + 256] = jnp.concatenate([k0, k1, k2, z], 1).astype(BF16)
        w3n[128:256, n * 256 : n * 256 + 256] = jnp.concatenate([z, k0, k1, k2], 1).astype(BF16)

    tt[...] = jnp.zeros_like(tt)

    def load_plane(src, half, scale):
        def step(i):
            x = src[pl.ds(i * 8, 8)].astype(F32)
            if scale is not None:
                x = x * scale
            vs[pl.ds(half * 1024 + i * 128, 128), :] = x.reshape(128, 128)

        loop(8, step)

    def turn(j):
        def step(i):
            for u in range(4):
                h = i * 4 + u
                tt[u, 8:136] = vs[pl.ds(h, 128, 16), :].T
                for kw in range(3):
                    xt[kw, j, h + 1] = tt[u, 7 + kw : 135 + kw].astype(BF16)

        loop(4, step)

    def rows_out(n, js, count):
        up = remote(xt.at[1, pl.ds(js, count), 16], rr.at[0, pl.ds(js, count)], rs.at[n, 0], rrs.at[n, 0], gx, yup)
        dn = remote(xt.at[1, pl.ds(js, count), 1], rr.at[1, pl.ds(js, count)], rs.at[n, 1], rrs.at[n, 1], gx, ydn)
        return up, dn

    def place_row(d, j):
        tt[0, 8:136] = rr[d, j].astype(F32) * (has_ydn if d == 0 else has_yup)
        for kw in range(3):
            xt[kw, j, 17 * d] = tt[0, 7 + kw : 135 + kw].astype(BF16)

    local_vol.wait()
    for j in (1, 2):
        load_plane(v.at[2 * j - 1], 0, None)
        load_plane(v.at[2 * j], 1, None)
        turn(j)
    inner = rows_out(0, 1, 2)
    for c in inner:
        c.start()

    def section3(j, half):
        top = 8 * half
        acc = None
        for kh in range(3):
            parts = []
            for kw in range(3):
                parts.append(xt[kw, j, pl.ds(top + kh, 8)].reshape(1024, 128))
                parts.append(xt[kw, j + 1, pl.ds(top + kh, 8)].reshape(1024, 128))
            d = lax.dot_general(
                jnp.concatenate(parts, 1), w3n[:, kh * 768 : (kh + 1) * 768], NT, preferred_element_type=F32
            )
            acc = d if acc is None else acc + d
        m = jnp.maximum(acc[:, :128], acc[:, 128:]).reshape(4, 2, 128, 128)
        bias = b3[...].astype(F32)
        for q in range(4):
            pt[q] = jnp.maximum(m[q, 0], m[q, 1])
            p = jnp.maximum(pt[q, pl.ds(0, 64, 2), :], pt[q, pl.ds(1, 64, 2), :])
            place_pooled(jnp.maximum(p + bias, 0.0), j + 1, half * 4 + q + 1)

    def place_pooled(p, plane, r):
        z = jnp.zeros((1, 128), F32)
        x4[0, plane, r] = jnp.concatenate([z, p[:-1]], 0).astype(BF16)
        x4[1, plane, r] = p.astype(BF16)
        x4[2, plane, r] = jnp.concatenate([p[1:], z], 0).astype(BF16)

    for c in inner:
        c.wait_recv()
    for j in (1, 2):
        for d in range(2):
            place_row(d, j)
    section3(1, 0)

    loop(NX - 1, lambda k: gather_x_in(k).wait_recv())
    lane_group = lax.broadcasted_iota(jnp.int32, (16, 128), 1) // 8

    def swap(q):
        a = [ga[i, pl.ds(pl.multiple_of(q * 16, 16), 16)].astype(F32) for i in range(16)]
        for s in (1, 2, 4, 8):
            low = (lane_group // s) % 2 == 0
            nxt = list(a)
            for i in range(16):
                if i & s == 0:
                    nxt[i] = jnp.where(low, a[i], pltpu.roll(a[i + s], 8 * s, 1))
                    nxt[i + s] = jnp.where(low, pltpu.roll(a[i], 128 - 8 * s, 1), a[i + s])
            a = nxt
        base = lax.rem(q, 2) * 512 + (q // 2) * 16
        for b in range(16):
            ff[pl.ds(base + b, 16, 32), :] = a[b]

    loop(4, swap)
    mine = pl.ds(pl.multiple_of(gy * 32, 32), 32)

    def own_block(t):
        wk[t, mine, :] = ff[pl.ds(pl.multiple_of(t * 32, 32), 32), :].astype(BF16)

    loop(28, own_block)

    def block(g):
        return wk.at[:, pl.ds(pl.multiple_of(g * 32, 32), 32), :]

    def gather_y(k):
        return remote(block(gy), block(gy), bs.at[k], br.at[k], gx, lax.rem(gy + 2 * k, NY))

    def gather_y_in(k):
        return remote(
            block(lax.rem(gy + NY - 2 * k, NY)), block(lax.rem(gy + NY - 2 * k, NY)), bs.at[k], br.at[k], gx, sib
        )

    def pass_on(k):
        src = lax.rem(gy + NY - 2 * k, NY)
        return remote(block(src), block(src), fs.at[k], fr.at[k], gx, sib)

    def pass_in(k):
        src = lax.rem(sib + NY - 2 * k, NY)
        return remote(block(src), block(src), fs.at[k], fr.at[k], gx, sib)

    for k in (2, 1, 3):
        gather_y(k).start()
    pass_on(0).start()

    plane_up.wait_recv()
    load_plane(rh.at[0], 0, has_xdn)
    load_plane(v.at[0], 1, None)
    turn(0)
    first = rows_out(1, 0, 1)
    for c in first:
        c.start()
    plane_dn.wait_recv()
    load_plane(v.at[5], 0, None)
    load_plane(rh.at[1], 1, has_xup)
    turn(3)
    last = rows_out(2, 3, 1)
    for c in last:
        c.start()
    section3(1, 1)
    for c in first:
        c.wait_recv()
    for d in range(2):
        place_row(d, 0)
    section3(0, 0)
    section3(0, 1)
    pooled_dn = remote(x4.at[1, 1, pl.ds(1, 8)], ph.at[1], phs.at[1], phr.at[1], xdn, gy)
    pooled_dn.start()
    for c in last:
        c.wait_recv()
    for d in range(2):
        place_row(d, 3)
    section3(2, 0)
    section3(2, 1)
    pooled_up = remote(x4.at[1, 3, pl.ds(1, 8)], ph.at[0], phs.at[0], phr.at[0], xup, gy)
    pooled_up.start()

    def pooled_rows(n, plane, count):
        up = remote(x4.at[1, pl.ds(plane, count), 8], pr.at[0, pl.ds(plane, count)], prs.at[n, 0], prr.at[n, 0], gx, yup)
        dn = remote(x4.at[1, pl.ds(plane, count), 1], pr.at[1, pl.ds(plane, count)], prs.at[n, 1], prr.at[n, 1], gx, ydn)
        return up, dn

    def place_pooled_row(d, plane):
        place_pooled(pr[d, plane].astype(F32) * (has_ydn if d == 0 else has_yup), plane, 9 * d)

    mid = pooled_rows(0, 1, 3)
    for c in mid:
        c.start()
    for k in (1, 3, 2):
        gather_y_in(k).wait_recv()
        pass_on(k).start()

    pooled_dn.wait_recv()
    loop(8, lambda r: place_pooled(ph[1, r].astype(F32) * has_xup, 4, r + 1))
    high = pooled_rows(2, 4, 1)
    for c in high:
        c.start()
    pooled_up.wait_recv()
    loop(8, lambda r: place_pooled(ph[0, r].astype(F32) * has_xdn, 0, r + 1))
    low = pooled_rows(1, 0, 1)
    for c in low:
        c.start()
    for c in mid:
        c.wait_recv()
    for plane in (1, 2, 3):
        for d in range(2):
            place_pooled_row(d, plane)
    for k in (0, 1, 3, 2):
        pass_in(k).wait_recv()

    def send_out(d, k):
        to = lax.rem(gy + k + 1, NY)
        return remote(
            ob.at[d, pl.ds(pl.multiple_of(to * 32, 32), 32)],
            out.at[d, :, pl.ds(pl.multiple_of(gy * 512, 512), 512)],
            os_.at[d, k], or_.at[d, k], gx, to,
        )

    def come_in(d, k):
        src = lax.rem(gy + NY - k - 1, NY)
        return remote(
            ob.at[d, pl.ds(pl.multiple_of(gy * 32, 32), 32)],
            out.at[d, :, pl.ds(pl.multiple_of(src * 512, 512), 512)],
            os_.at[d, k], or_.at[d, k], gx, src,
        )

    def keep(d):
        return pltpu.make_async_copy(
            ob.at[d, pl.ds(pl.multiple_of(gy * 32, 32), 32)],
            out.at[d, :, pl.ds(pl.multiple_of(gy * 512, 512), 512)],
            ol.at[d],
        )

    def section4(d):
        hot = jnp.where(lax.broadcasted_iota(jnp.int32, (512, 128), 1) == 0, 1.0, 0.0).astype(BF16)
        acc = None
        for t in range(0, 28, 2):
            xs = []
            for u in (t, t + 1):
                kd, kh, kw = u // 9, u // 3 % 3, u % 3
                xs.append(hot if u == 27 else x4[kw, d + kd, pl.ds(kh, 8)].reshape(512, 128))
            part = lax.dot_general(
                jnp.concatenate([wk[t], wk[t + 1]], 1), jnp.concatenate(xs, 1), NT, preferred_element_type=F32
            )
            acc = part if acc is None else acc + part
        ob[d] = jnp.where(acc > 0, acc, 0.3 * acc).astype(BF16)
        loop(NY - 1, lambda k: send_out(d, k).start())
        keep(d).start()

    section4(1)
    for c in low:
        c.wait_recv()
    for d in range(2):
        place_pooled_row(d, 0)
    section4(0)
    for c in high:
        c.wait_recv()
    for d in range(2):
        place_pooled_row(d, 4)
    section4(2)

    for c in (plane_up, plane_dn, *inner, *first, *last, pooled_up, pooled_dn, *mid, *low, *high):
        c.wait_send()
    loop(NX - 1, lambda k: gather_x(k).wait_send())
    for k in (1, 2, 3):
        gather_y(k).wait_send()
    for k in (0, 1, 2, 3):
        pass_on(k).wait_send()
    for d in (1, 0, 2):
        loop(NY - 1, lambda k: send_out(d, k).wait_send())
        keep(d).wait()
    for d in (1, 0, 2):
        loop(NY - 1, lambda k: come_in(d, k).wait_recv())


def on_device(volume, weight3, bias3, weight4, bias4):
    vmem = pl.BlockSpec(memory_space=pltpu.VMEM)
    anywhere = pl.BlockSpec(memory_space=pl.ANY)
    dma = pltpu.SemaphoreType.DMA
    return pl.pallas_call(
        kernel,
        out_shape=jax.ShapeDtypeStruct((3, 32, 4096), BF16),
        in_specs=[anywhere, vmem, vmem, vmem, vmem],
        out_specs=anywhere,
        scratch_shapes=[
            pltpu.VMEM((6, 64, 16, 128), BF16),
            pltpu.VMEM((2, 64, 16, 128), BF16),
            pltpu.VMEM((2048, 128), F32),
            pltpu.VMEM((4, 144, 128), F32),
            pltpu.VMEM((3, 4, 18, 128, 128), BF16),
            pltpu.VMEM((2, 4, 128, 128), BF16),
            pltpu.VMEM((4096, 128), F32),
            pltpu.VMEM((256, 2304), BF16),
            pltpu.VMEM((3, 5, 10, 64, 128), BF16),
            pltpu.VMEM((2, 8, 64, 128), BF16),
            pltpu.VMEM((2, 5, 64, 128), BF16),
            pltpu.VMEM((4, 128, 128), F32),
            pltpu.VMEM((1024, 128), F32),
            pltpu.VMEM((16, 64, 128), BF16),
            pltpu.VMEM((1024, 128), F32),
            pltpu.VMEM((28, 256, 128), BF16),
            pltpu.VMEM((3, 256, 512), BF16),
            dma(()),
            dma((2,)), dma((2,)),
            dma((3, 2)), dma((3, 2)),
            dma((NX - 1,)), dma((NX - 1,)),
            dma((4,)), dma((4,)),
            dma((4,)), dma((4,)),
            dma((2,)), dma((2,)),
            dma((3, 2)), dma((3, 2)),
            dma((3, NY - 1)), dma((3, NY - 1)),
            dma((3,)),
        ],
        compiler_params=pltpu.CompilerParams(
            collective_id=0, has_side_effects=True, vmem_limit_bytes=58 * 2**20
        ),
        name="encoder",
    )(volume, weight3, bias3.reshape(1, 128), weight4, bias4.reshape(1, 32))


def solution(mesh):
    return jax.shard_map(
        on_device,
        mesh=mesh,
        in_specs=(P("gx", None, "gy", None), P(), P(), P("gy", None, "gx"), P("gy")),
        out_specs=P("gx", "gy", None),
        check_vma=False,
    )
```

time: 159 us -> 68.1 us (0.43); the launches traced: 155 us -> 67.9 us
  Pallas kernels: 0 us -> 60.5 us
  blocking collectives: 54.7 us -> 0 us
  starting transfers between devices: 28.1 us -> 0 us
  matrix products: 17.9 us -> 0 us
  other arithmetic: 17.1 us -> 0 us
  between operations: 14.4 us -> 0.01 us
  local copies, waits for them, and re-layouts: 17.1 us -> 7.32 us
  waiting for transfers between devices: 6.06 us -> 0 us
    pallas_call x0 -> x1, Pallas kernels: none -> 60.5 us  [on_device(): pl.pallas_call(kernel, out_shape=jax.ShapeDtypeStruct((3, 32, 4096), BF16...]
    ppermute x8 -> x0, starting transfers between devices: 28.1 us -> none  [the longest x4 21.7 us: with_halo(): lax.ppermute(lax.slice_in_dim(block, block.shape[dim] - width, None, axis...]
    all_gather x1 -> x0, blocking collectives: 22.8 us -> none  [on_device(): kernel_in = lax.all_gather(weight4, 'gx', axis=2, tiled=True)]
    all_to_all x1 -> x0, blocking collectives: 19.3 us -> none  [on_device(): lax.all_to_all(local, 'gy', split_axis=1, concat_axis=2, tiled=True)]
    conv_general_dilated x2 -> x0, matrix products: 17.9 us -> none  [block_conv(): lax.conv_general_dilated(padded[None], kernel, (1, 1, 1), 'VALID', dimens...]
    unnamed x1 -> x0, blocking collectives: 12.5 us -> none
    broadcast_in_dim x2 -> x0, other arithmetic: 8.73 us -> none  [block_conv(): padded[None]]
    ppermute x8 -> x0, waiting for transfers between devices: 6.02 us -> none  [the longest x4 5.39 us: with_halo(): lax.ppermute(lax.slice_in_dim(block, 0, width, axis=dim), axis, backward)]
  transfers between devices with their start and end apart: 9 -> 0, of which waited for: 3 -> 0; matrix products, arithmetic and copies ran while one was open for 25% -> 0% of each run, Pallas kernels for 0% -> 0%
where the time goes in v1:
time: 68.1 us; the launch traced here: 67.9 us
  Pallas kernels  60.5 us (89%)
  local copies, waits for them, and re-layouts  7.32 us (11%)
    pallas_call x1, Pallas kernels, on_device(): pl.pallas_call(kernel, out_shape=jax.ShapeDtypeStruct((3, 32, 4096), BF16...  60.5 us
    unnamed x3, local copies, waits for them, and re-layouts  7.32 us

profile of v1, /device:TPU:1, one launch (start us, length us, event | category | flops | bytes accessed | tf_op | source)
XLA Modules:
  0.0 67.9 jit_solution(16274429033712373029)
XLA Ops:
  0.0 1.9 %copy.7.w4 = bf16[32,27,8]{2,1,0:T(8,128)(2,1)} copy(bf16[32,27,8]{0,2,1:T(8,128)(2,1)} %param.8) | data formatting | bytes 27648 | tf_op args[3]
  1.9 3.3 %copy.6.w3 = bf16[128,27,64]{2,1,0:T(8,128)(2,1)} copy(bf16[128,27,64]{0,2,1:T(8,128)(2,1)} %param.6) | data formatting | bytes 884736 | tf_op args[1]
  5.3 60.5 %encoder.1 = bf16[3,32,4096]{2,1,0:T(8,128)(2,1)} custom-call(bf16[6,64,16,128]{3,2,1,0:T(8,128)(2,1)} %vol.1, bf16[128,27,64]{2,1,0:T(8,128)(2,1)} %copy.6.w3, bf16[1,128]{1,0:T(2,128)(2,1)} %bitcast.2, bf16[32,27,8]{2,1,0:T(8,128)(2,1)} %copy.7.w4, bf16[1,32]{1,0:T(2,128)(2,1)} %bitcast.3), custom_call_target="tpu_custom_call" | custom-call | tf_op jit(solution)/shard_map/encoder/pallas_call | solution.py:354
  65.8 2.1 %copy.9 = bf16[3,32,4096]{2,1,0:T(8,128)(2,1)} copy(bf16[3,32,4096]{2,1,0:T(8,128)(2,1)} %encoder.1) | data formatting | bytes 1572864

commit v2 on v0

v2 whole, which is shorter than its diff:
```python
import jax
import jax.numpy as jnp
from jax import lax
from jax.experimental import pallas as pl
from jax.experimental.pallas import tpu as pltpu
from jax.sharding import PartitionSpec as P

MESH = pl.DeviceIdType.MESH
F32 = jnp.float32
BF16 = jnp.bfloat16
NT = (((1,), (1,)), ((), ()))
NN = (((1,), (0,)), ((), ()))
NX = 16
NY = 8


def remote(src, dst, send, recv, gx, gy):
    return pltpu.make_async_remote_copy(
        src_ref=src, dst_ref=dst, send_sem=send, recv_sem=recv, device_id=(gx, gy), device_id_type=MESH
    )


def loop(count, step):
    lax.fori_loop(0, count, lambda i, c: (step(i), c)[1], 0)


def kernel(
    vol, w3, b3, w4, b4, out,
    v, vs, tt, xt, q, rq, rr, rc, w3n, x4, ph, pr, pt, ws, ga, wk, ob,
    lsem, hs, hr, rs, rrs, as_, ar, bs, br, fs, fr, phs, phr, prs, prr, os_, or_, ol,
):
    gx = lax.axis_index("gx")
    gy = lax.axis_index("gy")
    xup, xdn = lax.rem(gx + 1, NX), lax.rem(gx + NX - 1, NX)
    yup, ydn = lax.rem(gy + 1, NY), lax.rem(gy + NY - 1, NY)
    sib = gy + 1 - 2 * lax.rem(gy, 2)
    has_xdn = (gx > 0).astype(F32)
    has_xup = (gx < NX - 1).astype(F32)
    has_ydn = (gy > 0).astype(F32)
    has_yup = (gy < NY - 1).astype(F32)

    barrier = pltpu.get_barrier_semaphore()

    def greet_x(k):
        pl.semaphore_signal(barrier, inc=1, device_id=(lax.rem(gx + k + 1, NX), gy), device_id_type=MESH)

    def greet_y(k):
        pl.semaphore_signal(barrier, inc=1, device_id=(gx, lax.rem(gy + k + 1, NY)), device_id_type=MESH)

    loop(NX - 1, greet_x)
    loop(NY - 1, greet_y)
    for dx in (xup, xdn):
        for dy in (yup, ydn):
            pl.semaphore_signal(barrier, inc=1, device_id=(dx, dy), device_id_type=MESH)
    local_vol = pltpu.make_async_copy(vol, v, lsem)
    local_vol.start()

    ws[...] = jnp.zeros_like(ws)
    ws[0:216, 0:32] = w4[...].astype(F32).reshape(216, 32)
    ws[216:217, 0:32] = b4[...].astype(F32)
    for t in range(2):
        ga[gx, t] = ws[t * 128 : (t + 1) * 128, :].T[0:32].astype(BF16)

    blank = jnp.zeros((64, 128), BF16)
    for n in range(9):
        for s in range(2):
            for p in range(4):
                tap = w3[9 * (p - s) + n] if 0 <= p - s < 3 else blank
                w3n[n * 256 + p * 64 : n * 256 + p * 64 + 64, s * 128 : (s + 1) * 128] = tap

    tt[...] = jnp.zeros_like(tt)

    def load_plane(src, half):
        def step(i):
            vs[pl.ds(half * 1024 + i * 128, 128), :] = src[pl.ds(i * 8, 8)].astype(F32).reshape(128, 128)

        loop(8, step)

    def place(x, u, j, h):
        tt[u, 8:136] = x
        for kw in range(3):
            xt[kw, j, h] = tt[u, 7 + kw : 135 + kw].astype(BF16)

    def turn(j):
        def step(i):
            for u in range(4):
                h = i * 4 + u
                place(vs[pl.ds(h, 128, 16), :].T, u, j, h + 1)

        loop(4, step)

    def turn_outer(n):
        def step(i):
            for u in range(2):
                r = i * 2 + u
                pair = jnp.concatenate(
                    [vs[pl.ds(n * 1024 + 2 * r, 64, 16), :], vs[pl.ds(n * 1024 + 2 * r + 1, 64, 16), :]], 0
                )
                q[n, r] = pair.T.astype(BF16)

        loop(4, step)

    left = lax.broadcasted_iota(jnp.int32, (128, 128), 1) < 64

    def merge(lo, hi, odd):
        if odd:
            return jnp.where(left, pltpu.roll(lo, 64, 1), hi)
        return jnp.where(left, lo, pltpu.roll(hi, 64, 1))

    local_vol.wait()
    for j in (1, 2):
        load_plane(v.at[2 * j - 1], 0)
        load_plane(v.at[2 * j], 1)
        turn(j)
    for n in range(2):
        load_plane(v.at[5 * n], n)
    for n in range(2):
        turn_outer(n)

    def section3(j, tops):
        def rows(kw, p, kh):
            if len(tops) == 1:
                return xt[kw, p, pl.ds(2 * tops[0] + kh, 8)].reshape(1024, 128)
            return jnp.concatenate([xt[kw, p, pl.ds(2 * t + kh, 4)].reshape(512, 128) for t in tops], 0)

        acc = None
        for kh in range(3):
            parts = []
            for kw in range(3):
                parts.append(rows(kw, j, kh))
                parts.append(rows(kw, j + 1, kh))
            d = lax.dot_general(
                jnp.concatenate(parts, 1), w3n[kh * 768 : (kh + 1) * 768, :], NN, preferred_element_type=F32
            )
            acc = d if acc is None else acc + d
        m = jnp.maximum(acc[:, :128], acc[:, 128:]).reshape(4, 2, 128, 128)
        bias = b3[...].astype(F32)
        for i in range(4):
            pt[i] = jnp.maximum(m[i, 0], m[i, 1])
            p = jnp.maximum(pt[i, pl.ds(0, 64, 2), :], pt[i, pl.ds(1, 64, 2), :])
            place_pooled(jnp.maximum(p + bias, 0.0), j + 1, tops[0] + i + 1 if len(tops) == 1 else tops[i // 2] + i % 2 + 1)

    def place_pooled(p, plane, r):
        z = jnp.zeros((1, 128), F32)
        x4[0, plane, r] = jnp.concatenate([z, p[:-1]], 0).astype(BF16)
        x4[1, plane, r] = p.astype(BF16)
        x4[2, plane, r] = jnp.concatenate([p[1:], z], 0).astype(BF16)

    pl.semaphore_wait(barrier, NX - 1 + NY - 1 + 4)

    def planes_out(part):
        r = pl.ds(0, 5) if part == 0 else pl.ds(5, 3)
        up = remote(q.at[1, r], rq.at[0, r], hs.at[0, part], hr.at[0, part], xup, gy)
        dn = remote(q.at[0, r], rq.at[1, r], hs.at[1, part], hr.at[1, part], xdn, gy)
        return up, dn

    def rows_out(d):
        y = (yup, ydn)[d]
        r = (7, 0)[d]
        return (
            remote(xt.at[1, pl.ds(1, 2), (16, 1)[d]], rr.at[d], rs.at[0, d], rrs.at[0, d], gx, y),
            remote(q.at[:, r], rc.at[d, pl.ds(1, 2)], rs.at[1, d], rrs.at[1, d], gx, y),
            remote(q.at[1, r], rc.at[d, 0], rs.at[2, d], rrs.at[2, d], xup, y),
            remote(q.at[0, r], rc.at[d, 3], rs.at[3, d], rrs.at[3, d], xdn, y),
        )

    def gather_x(k):
        return remote(ga.at[gx], ga.at[gx], as_.at[k], ar.at[k], lax.rem(gx + k + 1, NX), gy)

    def gather_x_in(k):
        src = lax.rem(gx + NX - k - 1, NX)
        return remote(ga.at[src], ga.at[src], as_.at[k], ar.at[k], gx, gy)

    outer = [planes_out(0), planes_out(1)]
    edge = [rows_out(0), rows_out(1)]
    for d in range(2):
        edge[d][0].start()
    for c in outer[0]:
        c.start()
    loop(NX - 1, lambda k: gather_x(k).start())
    for d in range(2):
        for c in edge[d][1:]:
            c.start()
    for c in outer[1]:
        c.start()

    section3(1, (2,))
    for d in range(2):
        edge[d][0].wait_recv()
        for j in (1, 2):
            place(rr[d, j - 1].astype(F32) * (has_ydn, has_yup)[d], 2 * d + j - 1, j, 17 * d)
    section3(1, (0, 6))

    loop(NX - 1, lambda k: gather_x_in(k).wait_recv())
    lane_group = lax.broadcasted_iota(jnp.int32, (16, 128), 1) // 8

    def swap(q):
        t = q // 2
        half = pl.multiple_of(lax.rem(q, 2) * 16, 16)
        a = [ga[i, t, pl.ds(half, 16)].astype(F32) for i in range(16)]
        for s in (1, 2, 4, 8):
            low = (lane_group // s) % 2 == 0
            nxt = list(a)
            for i in range(16):
                if i & s == 0:
                    nxt[i] = jnp.where(low, a[i], pltpu.roll(a[i + s], 8 * s, 1))
                    nxt[i + s] = jnp.where(low, pltpu.roll(a[i], 128 - 8 * s, 1), a[i + s])
            a = nxt
        for i in range(16):
            wk[t * 16 + i, pl.ds(pl.multiple_of(gy * 32 + half, 16), 16), :] = a[i].astype(BF16)

    loop(4, swap)

    def block(g):
        return wk.at[pl.ds(0, 28), pl.ds(pl.multiple_of(g * 32, 32), 32), :]

    def gather_y(k):
        return remote(block(gy), block(gy), bs.at[k], br.at[k], gx, lax.rem(gy + 2 * k, NY))

    def gather_y_in(k):
        return remote(
            block(lax.rem(gy + NY - 2 * k, NY)), block(lax.rem(gy + NY - 2 * k, NY)), bs.at[k], br.at[k], gx, sib
        )

    def pass_on(k):
        src = lax.rem(gy + NY - 2 * k, NY)
        return remote(block(src), block(src), fs.at[k], fr.at[k], gx, sib)

    def pass_in(k):
        src = lax.rem(sib + NY - 2 * k, NY)
        return remote(block(src), block(src), fs.at[k], fr.at[k], gx, sib)

    for k in (2, 1, 3):
        gather_y(k).start()
    pass_on(0).start()

    def merge_rows(j, lo, hi):
        def step(r):
            for odd in range(2):
                x = merge(lo(r), hi(r), odd)
                place(x, odd + 2 * (j // 3), j, 2 * r + odd + 1)

        return step

    def span(first, count, step):
        lax.fori_loop(first, first + count, lambda i, c: (step(i), c)[1], 0)

    def outer_rows(first, count):
        span(first, count, merge_rows(0, lambda r: rq[0, r].astype(F32) * has_xdn, lambda r: q[0, r].astype(F32)))
        span(first, count, merge_rows(3, lambda r: q[1, r].astype(F32), lambda r: rq[1, r].astype(F32) * has_xup))

    def edge_rows(d):
        for c in edge[d][1:]:
            c.wait_recv()
        have = (has_ydn, has_yup)[d]
        b = [rc[d, i].astype(F32) for i in range(4)]
        place(merge(b[0] * (have * has_xdn), b[1] * have, d == 0), 0, 0, 17 * d)
        place(merge(b[2] * have, b[3] * (have * has_xup), d == 0), 1, 3, 17 * d)

    for c in outer[0]:
        c.wait_recv()
    outer_rows(0, 5)
    edge_rows(0)
    def pooled_plane(up, half):
        r = pl.ds(4 * half, 4)
        return remote(
            x4.at[1, 3 if up else 1, pl.ds(1 + 4 * half, 4)], ph.at[1 - up, r],
            phs.at[up, half], phr.at[up, half], xup if up else xdn, gy,
        )

    def pooled_rows(d):
        y = (yup, ydn)[d]
        r = (8, 1)[d]
        return (
            remote(x4.at[1, pl.ds(1, 3), r], pr.at[d, pl.ds(1, 3)], prs.at[0, d], prr.at[0, d], gx, y),
            remote(x4.at[1, 3, r], pr.at[d, 0], prs.at[1, d], prr.at[1, d], xup, y),
            remote(x4.at[1, 1, r], pr.at[d, 4], prs.at[2, d], prr.at[2, d], xdn, y),
        )

    def place_pooled_row(d, plane):
        have = has_yup if d else has_ydn
        if plane in (0, 4):
            have = have * (has_xup if plane else has_xdn)
        place_pooled(pr[d, plane].astype(F32) * have, plane, 9 * d)

    def place_pooled_plane(up, half):
        pooled_plane(up, half).wait_recv()
        have, plane = (has_xdn, 0) if up else (has_xup, 4)
        for i in range(4):
            r = half * 4 + i
            place_pooled(ph[1 - up, r].astype(F32) * have, plane, r + 1)

    rim = [pooled_rows(0), pooled_rows(1)]
    section3(0, (0,))
    pooled_plane(0, 0).start()
    section3(2, (0,))
    pooled_plane(1, 0).start()
    for c in rim[1]:
        c.start()
    for c in outer[1]:
        c.wait_recv()
    outer_rows(5, 3)
    edge_rows(1)
    section3(0, (4,))
    pooled_plane(0, 1).start()
    section3(2, (4,))
    rim[0][0].start()
    pooled_plane(1, 1).start()
    for c in rim[0][1:]:
        c.start()
    for k in (1, 3, 2):
        gather_y_in(k).wait_recv()
        pass_on(k).start()
    rim[1][0].wait_recv()
    for plane in (1, 2, 3):
        place_pooled_row(1, plane)
    for k in (0, 1, 3, 2):
        pass_in(k).wait_recv()

    def span_of(g, half):
        return pl.ds(pl.multiple_of(g * 512 + 256 * half, 256), 256)

    def result(d, half, g):
        return ob.at[d, half, pl.ds(pl.multiple_of(g * 32, 32), 32)]

    def send_out(d, half, k):
        to = lax.rem(gy + k + 1, NY)
        return remote(
            result(d, half, to), out.at[d, :, span_of(gy, half)], os_.at[d, half, k], or_.at[d, half, k], gx, to
        )

    def come_in(d, half, k):
        src = lax.rem(gy + NY - k - 1, NY)
        return remote(
            result(d, half, gy), out.at[d, :, span_of(src, half)], os_.at[d, half, k], or_.at[d, half, k], gx, src
        )

    def keep(d, half):
        return pltpu.make_async_copy(result(d, half, gy), out.at[d, :, span_of(gy, half)], ol.at[d, half])

    hot = jnp.where(lax.broadcasted_iota(jnp.int32, (256, 128), 1) == 0, 1.0, 0.0).astype(BF16)

    def section4(d, half):
        acc = None
        for t in range(0, 28, 2):
            xs = []
            for u in (t, t + 1):
                kd, kh, kw = u // 9, u // 3 % 3, u % 3
                xs.append(hot if u == 27 else x4[kw, d + kd, pl.ds(4 * half + kh, 4)].reshape(256, 128))
            part = lax.dot_general(
                jnp.concatenate([wk[t], wk[t + 1]], 1), jnp.concatenate(xs, 1), NT, preferred_element_type=F32
            )
            acc = part if acc is None else acc + part
        ob[d, half] = jnp.where(acc > 0, acc, 0.3 * acc).astype(BF16)
        loop(NY - 1, lambda k: send_out(d, half, k).start())
        keep(d, half).start()

    section4(1, 1)
    rim[0][0].wait_recv()
    for plane in (1, 2, 3):
        place_pooled_row(0, plane)
    section4(1, 0)
    place_pooled_plane(0, 0)
    place_pooled_plane(0, 1)
    rim[1][2].wait_recv()
    place_pooled_row(1, 4)
    section4(2, 1)
    rim[0][2].wait_recv()
    place_pooled_row(0, 4)
    section4(2, 0)
    place_pooled_plane(1, 0)
    place_pooled_plane(1, 1)
    rim[1][1].wait_recv()
    place_pooled_row(1, 0)
    section4(0, 1)
    rim[0][1].wait_recv()
    place_pooled_row(0, 0)
    section4(0, 0)

    for c in (*outer[0], *outer[1], *edge[0], *edge[1], *rim[0], *rim[1]):
        c.wait_send()
    for up in range(2):
        for half in range(2):
            pooled_plane(up, half).wait_send()
    loop(NX - 1, lambda k: gather_x(k).wait_send())
    for k in (1, 2, 3):
        gather_y(k).wait_send()
    for k in (0, 1, 2, 3):
        pass_on(k).wait_send()
    parts = [(d, half) for d in (1, 2, 0) for half in (1, 0)]
    for d, half in parts:
        loop(NY - 1, lambda k: send_out(d, half, k).wait_send())
        keep(d, half).wait()
    for d, half in parts:
        loop(NY - 1, lambda k: come_in(d, half, k).wait_recv())


def on_device(volume, weight3, bias3, weight4, bias4):
    vmem = pl.BlockSpec(memory_space=pltpu.VMEM)
    anywhere = pl.BlockSpec(memory_space=pl.ANY)
    dma = pltpu.SemaphoreType.DMA
    return pl.pallas_call(
        kernel,
        out_shape=jax.ShapeDtypeStruct((3, 32, 4096), BF16),
        in_specs=[anywhere, vmem, vmem, vmem, vmem],
        out_specs=anywhere,
        scratch_shapes=[
            pltpu.VMEM((6, 64, 16, 128), BF16),
            pltpu.VMEM((2048, 128), F32),
            pltpu.VMEM((4, 144, 128), F32),
            pltpu.VMEM((3, 4, 18, 128, 128), BF16),
            pltpu.VMEM((2, 8, 128, 128), BF16),
            pltpu.VMEM((2, 8, 128, 128), BF16),
            pltpu.VMEM((2, 2, 128, 128), BF16),
            pltpu.VMEM((2, 4, 128, 128), BF16),
            pltpu.VMEM((2304, 256), BF16),
            pltpu.VMEM((3, 5, 10, 64, 128), BF16),
            pltpu.VMEM((2, 8, 64, 128), BF16),
            pltpu.VMEM((2, 5, 64, 128), BF16),
            pltpu.VMEM((4, 128, 128), F32),
            pltpu.VMEM((256, 128), F32),
            pltpu.VMEM((16, 2, 32, 128), BF16),
            pltpu.VMEM((32, 256, 128), BF16),
            pltpu.VMEM((3, 2, 256, 256), BF16),
            dma(()),
            dma((2, 2)), dma((2, 2)),
            dma((4, 2)), dma((4, 2)),
            dma((NX - 1,)), dma((NX - 1,)),
            dma((4,)), dma((4,)),
            dma((4,)), dma((4,)),
            dma((2, 2)), dma((2, 2)),
            dma((3, 2)), dma((3, 2)),
            dma((3, 2, NY - 1)), dma((3, 2, NY - 1)),
            dma((3, 2)),
        ],
        compiler_params=pltpu.CompilerParams(
            collective_id=0, has_side_effects=True, vmem_limit_bytes=58 * 2**20
        ),
        name="encoder",
    )(volume, weight3.transpose(1, 2, 0), bias3.reshape(1, 128), weight4.transpose(1, 2, 0), bias4.reshape(1, 32))


def solution(mesh):
    return jax.shard_map(
        on_device,
        mesh=mesh,
        in_specs=(P("gx", None, "gy", None), P(), P(), P("gy", None, "gx"), P("gy")),
        out_specs=P("gx", "gy", None),
        check_vma=False,
    )
```

time: 159 us -> 51.9 us (0.33); the launches traced: 155 us -> 51.8 us
  blocking collectives: 54.7 us -> 0 us
  Pallas kernels: 0 us -> 49.7 us
  starting transfers between devices: 28.1 us -> 0 us
  matrix products: 17.9 us -> 0 us
  other arithmetic: 17.1 us -> 0 us
  local copies, waits for them, and re-layouts: 17.1 us -> 2.06 us
  between operations: 14.4 us -> 0.01 us
  waiting for transfers between devices: 6.06 us -> 0 us
    pallas_call x0 -> x1, Pallas kernels: none -> 49.7 us  [on_device(): pl.pallas_call(kernel, out_shape=jax.ShapeDtypeStruct((3, 32, 4096), BF16...]
    ppermute x8 -> x0, starting transfers between devices: 28.1 us -> none  [the longest x4 21.7 us: with_halo(): lax.ppermute(lax.slice_in_dim(block, block.shape[dim] - width, None, axis...]
    all_gather x1 -> x0, blocking collectives: 22.8 us -> none  [on_device(): kernel_in = lax.all_gather(weight4, 'gx', axis=2, tiled=True)]
    all_to_all x1 -> x0, blocking collectives: 19.3 us -> none  [on_device(): lax.all_to_all(local, 'gy', split_axis=1, concat_axis=2, tiled=True)]
    conv_general_dilated x2 -> x0, matrix products: 17.9 us -> none  [block_conv(): lax.conv_general_dilated(padded[None], kernel, (1, 1, 1), 'VALID', dimens...]
    unnamed x1 -> x0, blocking collectives: 12.5 us -> none
    broadcast_in_dim x2 -> x0, other arithmetic: 8.73 us -> none  [block_conv(): padded[None]]
    ppermute x8 -> x0, waiting for transfers between devices: 6.02 us -> none  [the longest x4 5.39 us: with_halo(): lax.ppermute(lax.slice_in_dim(block, 0, width, axis=dim), axis, backward)]
  transfers between devices with their start and end apart: 9 -> 0, of which waited for: 3 -> 0; matrix products, arithmetic and copies ran while one was open for 25% -> 0% of each run, Pallas kernels for 0% -> 0%
where the time goes in v2:
time: 51.9 us; the launch traced here: 51.8 us
  Pallas kernels  49.7 us (96%)
  local copies, waits for them, and re-layouts  2.06 us (4%)
    pallas_call x1, Pallas kernels, on_device(): pl.pallas_call(kernel, out_shape=jax.ShapeDtypeStruct((3, 32, 4096), BF16...  49.7 us
    unnamed x1, local copies, waits for them, and re-layouts  2.06 us

profile of v2, /device:TPU:1, one launch (start us, length us, event | category | flops | bytes accessed | tf_op | source)
XLA Modules:
  0.0 51.8 jit_solution(5200291457766536674)
XLA Ops:
  0.0 49.7 %encoder.1 = bf16[3,32,4096]{2,1,0:T(8,128)(2,1)} custom-call(bf16[6,64,16,128]{3,2,1,0:T(8,128)(2,1)} %vol.1, bf16[27,64,128]{2,1,0:T(8,128)(2,1)} %bitcast.4, bf16[1,128]{1,0:T(2,128)(2,1)} %bitcast.6, bf16[27,8,32]{2,1,0:T(8,128)(2,1)} %bitcast.5, bf16[1,32]{1,0:T(2,128)(2,1)} %bitcast.7), custom_call_target="tpu_custom_call" | custom-call | tf_op jit(solution)/shard_map/encoder/pallas_call | solution.py:402
  49.7 2.1 %copy.7 = bf16[3,32,4096]{2,1,0:T(8,128)(2,1)} copy(bf16[3,32,4096]{2,1,0:T(8,128)(2,1)} %encoder.1) | data formatting | bytes 1572864

commit v3 on v2

--- a/solution.py
+++ b/solution.py
@@ -61,13 +61,6 @@
     for t in range(2):
         ga[gx, t] = ws[t * 128 : (t + 1) * 128, :].T[0:32].astype(BF16)
 
-    blank = jnp.zeros((64, 128), BF16)
-    for n in range(9):
-        for s in range(2):
-            for p in range(4):
-                tap = w3[9 * (p - s) + n] if 0 <= p - s < 3 else blank
-                w3n[n * 256 + p * 64 : n * 256 + p * 64 + 64, s * 128 : (s + 1) * 128] = tap
-
     tt[...] = jnp.zeros_like(tt)
 
     def load_plane(src, half):
@@ -108,10 +101,6 @@
         return jnp.where(left, lo, pltpu.roll(hi, 64, 1))
 
     local_vol.wait()
-    for j in (1, 2):
-        load_plane(v.at[2 * j - 1], 0)
-        load_plane(v.at[2 * j], 1)
-        turn(j)
     for n in range(2):
         load_plane(v.at[5 * n], n)
     for n in range(2):
@@ -173,16 +162,28 @@
 
     outer = [planes_out(0), planes_out(1)]
     edge = [rows_out(0), rows_out(1)]
-    for d in range(2):
-        edge[d][0].start()
+    loop(NX - 1, lambda k: gather_x(k).start())
     for c in outer[0]:
         c.start()
-    loop(NX - 1, lambda k: gather_x(k).start())
     for d in range(2):
         for c in edge[d][1:]:
             c.start()
     for c in outer[1]:
         c.start()
+
+    for j in (1, 2):
+        load_plane(v.at[2 * j - 1], 0)
+        load_plane(v.at[2 * j], 1)
+        turn(j)
+    for d in range(2):
+        edge[d][0].start()
+
+    blank = jnp.zeros((64, 128), BF16)
+    for n in range(9):
+        for s in range(2):
+            for p in range(4):
+                tap = w3[9 * (p - s) + n] if 0 <= p - s < 3 else blank
+                w3n[n * 256 + p * 64 : n * 256 + p * 64 + 64, s * 128 : (s + 1) * 128] = tap
 
     section3(1, (2,))
     for d in range(2):

time: 51.9 us -> 50.2 us (0.967)
  Pallas kernels: 49.7 us -> 48 us
    pallas_call x1, Pallas kernels: 49.7 us -> 48 us  [on_device(): pl.pallas_call(kernel, out_shape=jax.ShapeDtypeStruct((3, 32, 4096), BF16...]
where the time goes in v3:
time: 50.2 us; the launch traced here: 50.1 us
  Pallas kernels  48 us (96%)
  local copies, waits for them, and re-layouts  2.06 us (4%)
    pallas_call x1, Pallas kernels, on_device(): pl.pallas_call(kernel, out_shape=jax.ShapeDtypeStruct((3, 32, 4096), BF16...  48 us
    unnamed x1, local copies, waits for them, and re-layouts  2.06 us

profile of v3, /device:TPU:1, one launch (start us, length us, event | category | flops | bytes accessed | tf_op | source)
XLA Modules:
  0.0 50.1 jit_solution(5192133140118227420)
XLA Ops:
  0.0 48.0 %encoder.1 = bf16[3,32,4096]{2,1,0:T(8,128)(2,1)} custom-call(bf16[6,64,16,128]{3,2,1,0:T(8,128)(2,1)} %vol.1, bf16[27,64,128]{2,1,0:T(8,128)(2,1)} %bitcast.4, bf16[1,128]{1,0:T(2,128)(2,1)} %bitcast.6, bf16[27,8,32]{2,1,0:T(8,128)(2,1)} %bitcast.5, bf16[1,32]{1,0:T(2,128)(2,1)} %bitcast.7), custom_call_target="tpu_custom_call" | custom-call | tf_op jit(solution)/shard_map/encoder/pallas_call | solution.py:403
  48.0 2.1 %copy.7 = bf16[3,32,4096]{2,1,0:T(8,128)(2,1)} copy(bf16[3,32,4096]{2,1,0:T(8,128)(2,1)} %encoder.1) | data formatting | bytes 1572864
